TPU v7x, 512 devices: a whole 4x8x8 slice. The times are simulated.
512 devices in a mesh: chan: 16 (over x, y_hi, core), tm: 32 (over z, y_lo).
Axes of the slice: x: 4, y: 8 (y_hi: 2, y_lo: 4; y = y_hi * 4 + y_lo), z: 8, core: 2. Of those that a mesh axis runs over, the one named last changes fastest.
Arguments:
- traces: bfloat16 [16, 128, 128, 512], P('chan', 'tm'), may hold values from -6 to 6
- pair_listed: int32 [16, 8], P('chan'), may hold values from 0 to 1, as said below
- owner_slot: int32 [16, 8], P('chan'), may hold values from 0 to 31, as said below
- window_count: int32 [16, 8, 32], P('chan'), may hold values from 1 to 4, as said below
Outputs:
- stacks: float32 [16, 32, 128, 128], P('chan', 'tm')
Inputs may be any that keep to these rules, and one draw needn't show every extreme that they name: `pair_listed`: every distance is listed for block 0. `owner_slot`: distinct within each block's row. `window_count`: the windows entering are the first ones of the group; 4 is reached in every draw.
All inputs are finite; a program needn't handle non-finite values.
Results may differ from a plain program's by a relative error of at most 0.015.
Values may be sent and summed in bfloat16 or wider, within the bound.
No kernel may reach another device: no remote copies, remote signals or barrier semaphores. Data moves between devices by JAX's collectives and lax.ppermute only.
A program may use at most 64 MiB of HBM per device.

v0:
```python
import math
import jax
import jax.numpy as jnp
from jax import lax
from jax.sharding import PartitionSpec as P

BAND = 64
SMOOTH = 16
OFFSETS = 128
LAGS = 128
WATER = 0.1
PRECISE = lax.Precision.HIGHEST


def passed_along(block, axis, distance):
    devices = range(lax.axis_size(axis))
    route = [((i - distance) % len(devices), i) for i in devices]
    return lax.ppermute(block, axis, route)


def angles(left_index, right_index, period):
    product = left_index[:, None] * right_index[None, :] % period
    return 2.0 * math.pi / period * product.astype(jnp.float32)


def smooth_matrix():
    source = jnp.arange(BAND, dtype=jnp.int32)[:, None]
    target = jnp.arange(BAND, dtype=jnp.int32)[None, :]
    start = jnp.clip(target - SMOOTH // 2, 0, BAND - SMOOTH)
    inside = (source >= start) & (source < start + SMOOTH)
    return inside.astype(jnp.float32) / SMOOTH


def split_table(table):
    table_high = table.astype(jnp.bfloat16)
    table_low = (table - table_high.astype(jnp.float32)).astype(jnp.bfloat16)
    return (table_high, table_low)


def whiten(traces_local):
    windows, channels, samples = traces_local.shape
    flat_rows = traces_local.reshape(windows * channels, samples)
    phase_turn = angles(
        jnp.arange(samples, dtype=jnp.int32), jnp.arange(BAND, dtype=jnp.int32) + 1, samples
    )
    band_table = jnp.concatenate([jnp.cos(phase_turn), -jnp.sin(phase_turn)], axis=1)
    table_high, table_low = split_table(band_table)
    spectrum = jnp.dot(flat_rows, table_high, preferred_element_type=jnp.float32)
    spectrum = spectrum + jnp.dot(flat_rows, table_low, preferred_element_type=jnp.float32)
    real_part = spectrum[:, :BAND]
    imag_part = spectrum[:, BAND:]
    amplitude = jnp.sqrt(real_part * real_part + imag_part * imag_part)
    local_mean = jnp.dot(amplitude, smooth_matrix(), precision=PRECISE)
    water_level = local_mean + WATER * jnp.mean(amplitude, axis=1, keepdims=True) + 1e-06
    whitened = spectrum / jnp.concatenate([water_level, water_level], axis=1)
    return whitened.astype(jnp.bfloat16).reshape(windows, channels, 2 * BAND)


def channel_spectrum(block_data):
    channels = block_data.shape[1]
    padded = 2 * channels
    phase_turn = angles(
        jnp.arange(channels, dtype=jnp.int32), jnp.arange(padded, dtype=jnp.int32), padded
    )
    cos_high, cos_low = split_table(jnp.cos(phase_turn))
    sin_high, sin_low = split_table(jnp.sin(phase_turn))
    with_cos = jnp.einsum("wcg,ck->wkg", block_data, cos_high, preferred_element_type=jnp.float32)
    with_cos = with_cos + jnp.einsum(
        "wcg,ck->wkg", block_data, cos_low, preferred_element_type=jnp.float32
    )
    with_sin = jnp.einsum("wcg,ck->wkg", block_data, sin_high, preferred_element_type=jnp.float32)
    with_sin = with_sin + jnp.einsum(
        "wcg,ck->wkg", block_data, sin_low, preferred_element_type=jnp.float32
    )
    spec_real = with_cos[..., :BAND] + with_sin[..., BAND:]
    spec_imag = with_cos[..., BAND:] - with_sin[..., :BAND]
    return (spec_real, spec_imag)


def pair_term(arrived, own_real, own_imag, window_used, weight):
    src_real, src_imag = channel_spectrum(arrived)
    windows = arrived.shape[0]
    window_keep = (jnp.arange(windows, dtype=jnp.int32) < window_used).astype(jnp.float32)[
        :, None, None
    ]
    cross_real = jnp.sum(window_keep * (src_real * own_real + src_imag * own_imag), axis=0)
    cross_imag = jnp.sum(window_keep * (src_real * own_imag - src_imag * own_real), axis=0)
    padded = cross_real.shape[0]
    offset_steps = jnp.arange(OFFSETS, dtype=jnp.int32) - OFFSETS // 2
    phase_turn = angles(offset_steps, jnp.arange(padded, dtype=jnp.int32), padded)
    back_cos = jnp.cos(phase_turn) / padded
    back_sin = jnp.sin(phase_turn) / padded
    part_real = jnp.dot(back_cos, cross_real, precision=PRECISE) - jnp.dot(
        back_sin, cross_imag, precision=PRECISE
    )
    part_imag = jnp.dot(back_sin, cross_real, precision=PRECISE) + jnp.dot(
        back_cos, cross_imag, precision=PRECISE
    )
    return weight * jnp.concatenate([part_real, part_imag], axis=1)


def shards(traces, pair_listed, owner_slot, window_count):
    samples = traces.shape[3]
    whitened = whiten(traces[0])
    own_real, own_imag = channel_spectrum(whitened)
    pair_span = pair_listed.shape[1]
    groups = window_count.shape[2]
    group_index = lax.axis_index("tm")
    picked = jnp.arange(groups, dtype=jnp.int32) == group_index
    counts_here = jnp.sum(jnp.where(picked[None, :], window_count[0], 0), axis=1)
    totals = jnp.sum(window_count[0], axis=1).astype(jnp.float32)
    weights = pair_listed[0].astype(jnp.float32) / totals
    pair_terms = []
    moving = whitened
    for shift_step in range(pair_span):
        moving = passed_along(moving, "chan", 1)
        pair_terms.append(
            pair_term(moving, own_real, own_imag, counts_here[shift_step], weights[shift_step])
        )
    partials = jnp.stack(pair_terms)
    owners = owner_slot[0]
    summed = lax.psum(partials, "tm")
    owned_mask = (owners == group_index).astype(jnp.float32)
    owned = jnp.sum(owned_mask[:, None, None] * summed, axis=0)
    lag_angle = angles(
        jnp.arange(BAND, dtype=jnp.int32) + 1,
        jnp.arange(LAGS, dtype=jnp.int32) - LAGS // 2,
        samples,
    )
    lag_cos = jnp.cos(lag_angle)
    lag_sin = jnp.sin(lag_angle)
    stacked = jnp.dot(owned[:, :BAND], lag_cos, precision=PRECISE) - jnp.dot(
        owned[:, BAND:], lag_sin, precision=PRECISE
    )
    stacked = stacked / math.sqrt(BAND)
    return stacked[None, None]


def solution(mesh):
    placed = (P("chan", "tm", None, None), P("chan", None), P("chan", None), P("chan", None, None))
    return jax.shard_map(
        shards, mesh=mesh, in_specs=placed, out_specs=P("chan", "tm", None, None), check_vma=False
    )
```

profile of v0, /device:TPU:2, one launch (start us, length us, event | category | flops | bytes accessed | tf_op | source)
XLA Modules:
  0.0 484.5 jit_solution(13503771856990752241)
XLA Ops:
  6.6 1.1 fusion.35
  9.0 1.9 collective-permute-start
  17.3 1.2 compare_convert_fusion.1
  18.5 1.3 compare_convert_fusion.3
  24.0 7.8 %collective-permute-start.1 = (bf16[4,128,128]{1,2,0:T(8,128)(2,1)S(1)}, bf16[4,128,128]{1,2,0:T(8,128)(2,1)S(1)}, u32[]{:S(2)}, u32[]{:S(2)}) collective-permute-start(bf16[4,128,128]{1,2,0:T(8,128)(2,1)S(1)} %collective-permute-done), channel_id=1, source_target_pairs={{480,0},{0,32},{32,64},{64,96},{96,128},{128,160},{160,192},{192,2... | collective-permute-start | bytes 393224 | tf_op jit(solution)/shard_map/ppermute | solution.py:18
  31.9 3.3 collective-permute-done.1
  38.1 2.1 collective-permute-start.2
  40.2 8.9 %collective-permute-done.2 = bf16[4,128,128]{1,2,0:T(8,128)(2,1)S(1)} collective-permute-done((bf16[4,128,128]{1,2,0:T(8,128)(2,1)S(1)}, bf16[4,128,128]{1,2,0:T(8,128)(2,1)S(1)}, u32[]{:S(2)}, u32[]{:S(2)}) %collective-permute-start.2) | collective-permute-done | bytes 131104 | tf_op jit(solution)/shard_map/ppermute | solution.py:18
  52.0 1.9 collective-permute-start.3
  54.0 10.6 %collective-permute-done.3 = bf16[4,128,128]{1,2,0:T(8,128)(2,1)S(1)} collective-permute-done((bf16[4,128,128]{1,2,0:T(8,128)(2,1)S(1)}, bf16[4,128,128]{1,2,0:T(8,128)(2,1)S(1)}, u32[]{:S(2)}, u32[]{:S(2)}) %collective-permute-start.3) | collective-permute-done | bytes 131104 | tf_op jit(solution)/shard_map/ppermute | solution.py:18
  67.5 1.9 collective-permute-start.4
  69.5 9.2 %collective-permute-done.4 = bf16[4,128,128]{1,2,0:T(8,128)(2,1)S(1)} collective-permute-done((bf16[4,128,128]{1,2,0:T(8,128)(2,1)S(1)}, bf16[4,128,128]{1,2,0:T(8,128)(2,1)S(1)}, u32[]{:S(2)}, u32[]{:S(2)}) %collective-permute-start.4) | collective-permute-done | bytes 131104 | tf_op jit(solution)/shard_map/ppermute | solution.py:18
  81.6 1.9 collective-permute-start.5
  83.6 9.1 %collective-permute-done.5 = bf16[4,128,128]{1,2,0:T(8,128)(2,1)S(1)} collective-permute-done((bf16[4,128,128]{1,2,0:T(8,128)(2,1)S(1)}, bf16[4,128,128]{1,2,0:T(8,128)(2,1)S(1)}, u32[]{:S(2)}, u32[]{:S(2)}) %collective-permute-start.5) | collective-permute-done | bytes 131104 | tf_op jit(solution)/shard_map/ppermute | solution.py:18
  95.5 1.9 collective-permute-start.6
  97.5 9.1 %collective-permute-done.6 = bf16[4,128,128]{1,2,0:T(8,128)(2,1)S(1)} collective-permute-done((bf16[4,128,128]{1,2,0:T(8,128)(2,1)S(1)}, bf16[4,128,128]{1,2,0:T(8,128)(2,1)S(1)}, u32[]{:S(2)}, u32[]{:S(2)}) %collective-permute-start.6) | collective-permute-done | bytes 131104 | tf_op jit(solution)/shard_map/ppermute | solution.py:18
  109.5 2.3 collective-permute-start.7
  111.9 8.7 %collective-permute-done.7 = bf16[4,128,128]{1,2,0:T(8,128)(2,1)S(1)} collective-permute-done((bf16[4,128,128]{1,2,0:T(8,128)(2,1)S(1)}, bf16[4,128,128]{1,2,0:T(8,128)(2,1)S(1)}, u32[]{:S(2)}, u32[]{:S(2)}) %collective-permute-start.7) | collective-permute-done | bytes 131104 | tf_op jit(solution)/shard_map/ppermute | solution.py:18
  125.0 0.8 fusion.122
  125.9 0.8 fusion.115
  126.7 0.8 fusion.123
  128.8 0.8 fusion.124
  130.7 0.8 fusion.125
  132.3 0.8 fusion.126
  133.1 0.8 fusion.119
  134.0 0.8 fusion.127
  134.8 1.0 fusion.120
  135.8 0.8 fusion.128
  136.6 0.8 fusion.121
  138.3 0.8 fusion.7
  139.1 0.8 fusion.6
  139.9 0.8 fusion.9
  140.7 0.8 fusion.8
  141.6 0.8 fusion.11
  142.4 0.8 fusion.10
  143.2 0.8 fusion.13
  144.0 0.8 fusion.12
  144.9 0.8 fusion.15
  145.7 0.8 fusion.14
  146.5 0.8 fusion.17
  147.4 0.8 fusion.16
  148.2 0.8 fusion.19
  149.0 0.8 fusion.18
  149.8 0.8 fusion.4
  150.7 0.8 fusion.5
  157.4 317.5 %all-reduce.2.cloned.1.call-done = f32[8,128,128]{1,2,0:T(8,128)} async-done(((f32[8,128,128]{1,2,0:T(8,128)}), f32[8,128,128]{1,2,0:T(8,128)}) %all-reduce.2.cloned.1.call-update) | async-done | bytes 524304 | tf_op jit(solution)/shard_map/psum | solution.py:122
  474.9 1.2 multiply_reduce_fusion
  476.5 1.0 fusion.3
  (105 shorter events, 43.9 us)
Async XLA Ops:
  6.5 1.1 copy-start
  6.5 468.4 %all-reduce.2.cloned.1.call-start = ((), (), s32[]{:S(2)}) async-start(), calls=%async_computation | async-start | bytes 1048576 | tf_op jit(solution)/shard_map/psum | solution.py:122
  9.0 12.2 %collective-permute-start = (bf16[4,128,128]{1,2,0:T(8,128)(2,1)S(1)}, bf16[4,128,128]{1,2,0:T(8,128)(2,1)S(1)}, u32[]{:S(2)}, u32[]{:S(2)}) collective-permute-start(bf16[4,128,128]{1,2,0:T(8,128)(2,1)S(1)} %copy_bitcast_fusion), channel_id=1, source_target_pairs={{480,0},{0,32},{32,64},{64,96},{96,128},{128,160},{160,192},{192,2... | collective-permute-start | bytes 393224 | tf_op jit(solution)/shard_map/ppermute | solution.py:18
  13.7 0.7 copy-start.2
  18.5 1.3 copy-start.3
  24.0 11.2 %collective-permute-start.1 = (bf16[4,128,128]{1,2,0:T(8,128)(2,1)S(1)}, bf16[4,128,128]{1,2,0:T(8,128)(2,1)S(1)}, u32[]{:S(2)}, u32[]{:S(2)}) collective-permute-start(bf16[4,128,128]{1,2,0:T(8,128)(2,1)S(1)} %collective-permute-done), channel_id=1, source_target_pairs={{480,0},{0,32},{32,64},{64,96},{96,128},{128,160},{160,192},{192,2... | collective-permute-start | bytes 393224 | tf_op jit(solution)/shard_map/ppermute | solution.py:18
  38.1 11.1 %collective-permute-start.2 = (bf16[4,128,128]{1,2,0:T(8,128)(2,1)S(1)}, bf16[4,128,128]{1,2,0:T(8,128)(2,1)S(1)}, u32[]{:S(2)}, u32[]{:S(2)}) collective-permute-start(bf16[4,128,128]{1,2,0:T(8,128)(2,1)S(1)} %collective-permute-done.1), channel_id=1, source_target_pairs={{480,0},{0,32},{32,64},{64,96},{96,128},{128,160},{160,192},{192,2... | collective-permute-start | bytes 393224 | tf_op jit(solution)/shard_map/ppermute | solution.py:18
  52.0 12.6 %collective-permute-start.3 = (bf16[4,128,128]{1,2,0:T(8,128)(2,1)S(1)}, bf16[4,128,128]{1,2,0:T(8,128)(2,1)S(1)}, u32[]{:S(2)}, u32[]{:S(2)}) collective-permute-start(bf16[4,128,128]{1,2,0:T(8,128)(2,1)S(1)} %collective-permute-done.2), channel_id=1, source_target_pairs={{480,0},{0,32},{32,64},{64,96},{96,128},{128,160},{160,192},{192,2... | collective-permute-start | bytes 393224 | tf_op jit(solution)/shard_map/ppermute | solution.py:18
  67.5 11.2 %collective-permute-start.4 = (bf16[4,128,128]{1,2,0:T(8,128)(2,1)S(1)}, bf16[4,128,128]{1,2,0:T(8,128)(2,1)S(1)}, u32[]{:S(2)}, u32[]{:S(2)}) collective-permute-start(bf16[4,128,128]{1,2,0:T(8,128)(2,1)S(1)} %collective-permute-done.3), channel_id=1, source_target_pairs={{480,0},{0,32},{32,64},{64,96},{96,128},{128,160},{160,192},{192,2... | collective-permute-start | bytes 393224 | tf_op jit(solution)/shard_map/ppermute | solution.py:18
  81.6 11.1 %collective-permute-start.5 = (bf16[4,128,128]{1,2,0:T(8,128)(2,1)S(1)}, bf16[4,128,128]{1,2,0:T(8,128)(2,1)S(1)}, u32[]{:S(2)}, u32[]{:S(2)}) collective-permute-start(bf16[4,128,128]{1,2,0:T(8,128)(2,1)S(1)} %collective-permute-done.4), channel_id=1, source_target_pairs={{480,0},{0,32},{32,64},{64,96},{96,128},{128,160},{160,192},{192,2... | collective-permute-start | bytes 393224 | tf_op jit(solution)/shard_map/ppermute | solution.py:18
  95.5 11.1 %collective-permute-start.6 = (bf16[4,128,128]{1,2,0:T(8,128)(2,1)S(1)}, bf16[4,128,128]{1,2,0:T(8,128)(2,1)S(1)}, u32[]{:S(2)}, u32[]{:S(2)}) collective-permute-start(bf16[4,128,128]{1,2,0:T(8,128)(2,1)S(1)} %collective-permute-done.5), channel_id=1, source_target_pairs={{480,0},{0,32},{32,64},{64,96},{96,128},{128,160},{160,192},{192,2... | collective-permute-start | bytes 393224 | tf_op jit(solution)/shard_map/ppermute | solution.py:18
  109.5 11.1 %collective-permute-start.7 = (bf16[4,128,128]{1,2,0:T(8,128)(2,1)S(1)}, bf16[4,128,128]{1,2,0:T(8,128)(2,1)S(1)}, u32[]{:S(2)}, u32[]{:S(2)}) collective-permute-start(bf16[4,128,128]{1,2,0:T(8,128)(2,1)S(1)} %collective-permute-done.6), channel_id=1, source_target_pairs={{480,0},{0,32},{32,64},{64,96},{96,128},{128,160},{160,192},{192,2... | collective-permute-start | bytes 393224 | tf_op jit(solution)/shard_map/ppermute | solution.py:18
  156.6 0.8 copy-start.1
  156.6 0.8 copy-start.4
Sparse Core Ops, SparseCore 0:
  157.5 317.3 all-reduce.1
where the time goes:
time: 492 us; the launch traced here: 485 us
  waiting for transfers between devices  376 us (76%)
  matrix products  54 us (11%)
  starting transfers between devices  21.9 us (4%)
  other arithmetic  15.2 us (3%)
  between operations  14.3 us (3%)
    psum x1, waiting for transfers between devices, shards(): summed = lax.psum(partials, 'tm')  317 us
    ppermute x8, waiting for transfers between devices, passed_along(): return lax.ppermute(block, axis, route)  58.8 us
    unnamed x36, matrix products  24.8 us
    ppermute x8, starting transfers between devices, passed_along(): return lax.ppermute(block, axis, route)  21.9 us
  transfers between devices with their start and end apart: 9, of which 8 were waited for; matrix products, arithmetic and copies ran while one was open for 2% of the time, Pallas kernels for 0%

commit v1 on v0

--- a/solution.py
+++ b/solution.py
@@ -119,7 +119,8 @@
         )
     partials = jnp.stack(pair_terms)
     owners = owner_slot[0]
-    summed = lax.psum(partials, "tm")
+    parts = lax.all_gather(partials, "tm")
+    summed = jnp.sum(parts, axis=0)
     owned_mask = (owners == group_index).astype(jnp.float32)
     owned = jnp.sum(owned_mask[:, None, None] * summed, axis=0)
     lag_angle = angles(

time: 492 us -> 566 us (1.15)
  the two profiles are of different devices: /device:TPU:2 before, /device:TPU:1 now
where the time goes in v1:
time: 566 us; the launch traced here: 558 us
  waiting for transfers between devices  425 us (75%)
  matrix products  54.2 us (10%)
  starting transfers between devices  39.3 us (7%)
  other arithmetic  23.1 us (4%)
  between operations  14.3 us (3%)
    all_gather x1, waiting for transfers between devices, shards(): parts = lax.all_gather(partials, 'tm')  378 us
    ppermute x8, waiting for transfers between devices, passed_along(): return lax.ppermute(block, axis, route)  46.8 us
    ppermute x8, starting transfers between devices, passed_along(): return lax.ppermute(block, axis, route)  39.3 us
    unnamed x36, matrix products  24.8 us
  transfers between devices with their start and end apart: 9, of which 8 were waited for; matrix products, arithmetic and copies ran while one was open for 2% of the time, Pallas kernels for 0%

profile of v1, /device:TPU:1, one launch (start us, length us, event | category | flops | bytes accessed | tf_op | source)
XLA Modules:
  0.0 558.2 jit_solution(3429657423931642067)
XLA Ops:
  6.6 1.1 fusion.35
  9.0 8.8 %collective-permute-start = (bf16[4,128,128]{1,2,0:T(8,128)(2,1)S(1)}, bf16[4,128,128]{1,2,0:T(8,128)(2,1)S(1)}, u32[]{:S(2)}, u32[]{:S(2)}) collective-permute-start(bf16[4,128,128]{1,2,0:T(8,128)(2,1)S(1)} %copy_bitcast_fusion), channel_id=1, source_target_pairs={{480,0},{0,32},{32,64},{64,96},{96,128},{128,160},{160,192},{192,2... | collective-permute-start | bytes 393224 | tf_op jit(solution)/shard_map/ppermute | solution.py:18
  25.5 1.2 compare_convert_fusion.1
  26.7 1.3 compare_convert_fusion.3
  32.3 1.9 collective-permute-start.1
  34.3 1.9 collective-permute-done.1
  39.0 8.5 %collective-permute-start.2 = (bf16[4,128,128]{1,2,0:T(8,128)(2,1)S(1)}, bf16[4,128,128]{1,2,0:T(8,128)(2,1)S(1)}, u32[]{:S(2)}, u32[]{:S(2)}) collective-permute-start(bf16[4,128,128]{1,2,0:T(8,128)(2,1)S(1)} %collective-permute-done.1), channel_id=1, source_target_pairs={{480,0},{0,32},{32,64},{64,96},{96,128},{128,160},{160,192},{192,2... | collective-permute-start | bytes 393224 | tf_op jit(solution)/shard_map/ppermute | solution.py:18
  47.6 2.5 collective-permute-done.2
  53.0 7.4 %collective-permute-start.3 = (bf16[4,128,128]{1,2,0:T(8,128)(2,1)S(1)}, bf16[4,128,128]{1,2,0:T(8,128)(2,1)S(1)}, u32[]{:S(2)}, u32[]{:S(2)}) collective-permute-start(bf16[4,128,128]{1,2,0:T(8,128)(2,1)S(1)} %collective-permute-done.2), channel_id=1, source_target_pairs={{480,0},{0,32},{32,64},{64,96},{96,128},{128,160},{160,192},{192,2... | collective-permute-start | bytes 393224 | tf_op jit(solution)/shard_map/ppermute | solution.py:18
  60.5 4.8 collective-permute-done.3
  68.2 5.3 collective-permute-start.4
  73.5 7.0 %collective-permute-done.4 = bf16[4,128,128]{1,2,0:T(8,128)(2,1)S(1)} collective-permute-done((bf16[4,128,128]{1,2,0:T(8,128)(2,1)S(1)}, bf16[4,128,128]{1,2,0:T(8,128)(2,1)S(1)}, u32[]{:S(2)}, u32[]{:S(2)}) %collective-permute-start.4) | collective-permute-done | bytes 131104 | tf_op jit(solution)/shard_map/ppermute | solution.py:18
  83.3 3.2 collective-permute-start.5
  86.6 9.1 %collective-permute-done.5 = bf16[4,128,128]{1,2,0:T(8,128)(2,1)S(1)} collective-permute-done((bf16[4,128,128]{1,2,0:T(8,128)(2,1)S(1)}, bf16[4,128,128]{1,2,0:T(8,128)(2,1)S(1)}, u32[]{:S(2)}, u32[]{:S(2)}) %collective-permute-start.5) | collective-permute-done | bytes 131104 | tf_op jit(solution)/shard_map/ppermute | solution.py:18
  98.5 1.9 collective-permute-start.6
  100.5 10.3 %collective-permute-done.6 = bf16[4,128,128]{1,2,0:T(8,128)(2,1)S(1)} collective-permute-done((bf16[4,128,128]{1,2,0:T(8,128)(2,1)S(1)}, bf16[4,128,128]{1,2,0:T(8,128)(2,1)S(1)}, u32[]{:S(2)}, u32[]{:S(2)}) %collective-permute-start.6) | collective-permute-done | bytes 131104 | tf_op jit(solution)/shard_map/ppermute | solution.py:18
  113.7 2.3 collective-permute-start.7
  116.1 11.3 %collective-permute-done.7 = bf16[4,128,128]{1,2,0:T(8,128)(2,1)S(1)} collective-permute-done((bf16[4,128,128]{1,2,0:T(8,128)(2,1)S(1)}, bf16[4,128,128]{1,2,0:T(8,128)(2,1)S(1)}, u32[]{:S(2)}, u32[]{:S(2)}) %collective-permute-start.7) | collective-permute-done | bytes 131104 | tf_op jit(solution)/shard_map/ppermute | solution.py:18
  130.6 0.8 fusion.121
  134.3 0.8 fusion.127
  135.2 0.8 fusion.119
  136.0 0.8 fusion.128
  136.8 0.8 fusion.120
  138.1 0.8 fusion.122
  139.8 0.8 fusion.123
  140.6 0.8 fusion.115
  141.4 1.0 fusion.126
  143.4 0.8 fusion.125
  145.1 0.8 fusion.5
  145.9 0.8 fusion.4
  146.7 0.8 fusion.11
  147.6 0.8 fusion.10
  148.4 0.8 fusion.17
  149.2 0.8 fusion.16
  150.0 0.8 fusion.19
  150.9 0.8 fusion.18
  151.7 0.8 fusion.7
  152.5 0.8 fusion.6
  153.4 0.8 fusion.9
  154.2 0.8 fusion.8
  155.0 0.8 fusion.15
  155.8 0.8 fusion.14
  156.7 1.0 fusion.13
  157.7 0.8 fusion.12
  163.6 1.0 copy.22
  164.6 377.8 %all-gather.3.cloned.1.call-done = f32[256,128,128]{2,1,0:T(8,128)} async-done(((f32[8,128,128]{2,1,0:T(8,128)}), f32[256,128,128]{2,1,0:T(8,128)}) %all-gather.3.cloned.1.call-update) | async-done | bytes 16777232 | tf_op jit(solution)/shard_map/all_gather | solution.py:122
  542.5 6.9 %reduce_sum.208 = f32[8,128,128]{2,1,0:T(8,128)S(1)} reduce(f32[32,8,128,128]{3,2,1,0:T(8,128)} %bitcast.292, f32[]{:T(128)} %constant.125.clone.1), dimensions={0}, to_apply=%region_19.20 | reduce | flops 4063232 | bytes 17301508 | tf_op jit(solution)/shard_map/reduce_sum | solution.py:123
  550.1 1.0 fusion.3
  (102 shorter events, 45.6 us)
Async XLA Ops:
  6.5 1.1 copy-start
  6.5 535.9 %all-gather.3.cloned.1.call-start = ((), (), s32[]{:S(2)}) async-start(), calls=%async_computation | async-start | bytes 17301504 | tf_op jit(solution)/shard_map/all_gather | solution.py:122
  9.0 20.4 %collective-permute-start = (bf16[4,128,128]{1,2,0:T(8,128)(2,1)S(1)}, bf16[4,128,128]{1,2,0:T(8,128)(2,1)S(1)}, u32[]{:S(2)}, u32[]{:S(2)}) collective-permute-start(bf16[4,128,128]{1,2,0:T(8,128)(2,1)S(1)} %copy_bitcast_fusion), channel_id=1, source_target_pairs={{480,0},{0,32},{32,64},{64,96},{96,128},{128,160},{160,192},{192,2... | collective-permute-start | bytes 393224 | tf_op jit(solution)/shard_map/ppermute | solution.py:18
  32.3 3.9 collective-permute-start.1
  39.0 11.1 %collective-permute-start.2 = (bf16[4,128,128]{1,2,0:T(8,128)(2,1)S(1)}, bf16[4,128,128]{1,2,0:T(8,128)(2,1)S(1)}, u32[]{:S(2)}, u32[]{:S(2)}) collective-permute-start(bf16[4,128,128]{1,2,0:T(8,128)(2,1)S(1)} %collective-permute-done.1), channel_id=1, source_target_pairs={{480,0},{0,32},{32,64},{64,96},{96,128},{128,160},{160,192},{192,2... | collective-permute-start | bytes 393224 | tf_op jit(solution)/shard_map/ppermute | solution.py:18
  53.0 12.3 %collective-permute-start.3 = (bf16[4,128,128]{1,2,0:T(8,128)(2,1)S(1)}, bf16[4,128,128]{1,2,0:T(8,128)(2,1)S(1)}, u32[]{:S(2)}, u32[]{:S(2)}) collective-permute-start(bf16[4,128,128]{1,2,0:T(8,128)(2,1)S(1)} %collective-permute-done.2), channel_id=1, source_target_pairs={{480,0},{0,32},{32,64},{64,96},{96,128},{128,160},{160,192},{192,2... | collective-permute-start | bytes 393224 | tf_op jit(solution)/shard_map/ppermute | solution.py:18
  68.2 12.3 %collective-permute-start.4 = (bf16[4,128,128]{1,2,0:T(8,128)(2,1)S(1)}, bf16[4,128,128]{1,2,0:T(8,128)(2,1)S(1)}, u32[]{:S(2)}, u32[]{:S(2)}) collective-permute-start(bf16[4,128,128]{1,2,0:T(8,128)(2,1)S(1)} %collective-permute-done.3), channel_id=1, source_target_pairs={{480,0},{0,32},{32,64},{64,96},{96,128},{128,160},{160,192},{192,2... | collective-permute-start | bytes 393224 | tf_op jit(solution)/shard_map/ppermute | solution.py:18
  83.3 12.3 %collective-permute-start.5 = (bf16[4,128,128]{1,2,0:T(8,128)(2,1)S(1)}, bf16[4,128,128]{1,2,0:T(8,128)(2,1)S(1)}, u32[]{:S(2)}, u32[]{:S(2)}) collective-permute-start(bf16[4,128,128]{1,2,0:T(8,128)(2,1)S(1)} %collective-permute-done.4), channel_id=1, source_target_pairs={{480,0},{0,32},{32,64},{64,96},{96,128},{128,160},{160,192},{192,2... | collective-permute-start | bytes 393224 | tf_op jit(solution)/shard_map/ppermute | solution.py:18
  98.5 12.3 %collective-permute-start.6 = (bf16[4,128,128]{1,2,0:T(8,128)(2,1)S(1)}, bf16[4,128,128]{1,2,0:T(8,128)(2,1)S(1)}, u32[]{:S(2)}, u32[]{:S(2)}) collective-permute-start(bf16[4,128,128]{1,2,0:T(8,128)(2,1)S(1)} %collective-permute-done.5), channel_id=1, source_target_pairs={{480,0},{0,32},{32,64},{64,96},{96,128},{128,160},{160,192},{192,2... | collective-permute-start | bytes 393224 | tf_op jit(solution)/shard_map/ppermute | solution.py:18
  113.7 13.7 %collective-permute-start.7 = (bf16[4,128,128]{1,2,0:T(8,128)(2,1)S(1)}, bf16[4,128,128]{1,2,0:T(8,128)(2,1)S(1)}, u32[]{:S(2)}, u32[]{:S(2)}) collective-permute-start(bf16[4,128,128]{1,2,0:T(8,128)(2,1)S(1)} %collective-permute-done.6), channel_id=1, source_target_pairs={{480,0},{0,32},{32,64},{64,96},{96,128},{128,160},{160,192},{192,2... | collective-permute-start | bytes 393224 | tf_op jit(solution)/shard_map/ppermute | solution.py:18
  130.3 34.3 %copy-start.1 = (s32[1,8]{1,0:T(1,128)S(1)}, s32[1,8]{1,0:T(1,128)}, u32[]{:S(2)}) copy-start(s32[1,8]{1,0:T(1,128)} %param.6) | copy-start | bytes 100
Sparse Core Ops, SparseCore 0:
  164.7 377.6 all-gather.2
